TPU v7x, 32 devices: a whole 2x2x4 slice. The times are simulated.
32 devices in a mesh: slab: 8 (over y, x, core), lat: 4 (over z).
Axes of the slice: x: 2, y: 2, z: 4, core: 2. Of those that a mesh axis runs over, the one named last changes fastest.
Arguments:
- nodes: bfloat16 [4096, 512], P('slab', 'lat')
- edges: bfloat16 [16384, 512], P(('slab', 'lat'))
- edge_tiles: int32 [2, 128], P(None, ('slab', 'lat')), may hold values from 0 to 7, as said below
- edge_offsets: int32 [2, 16384], P(None, ('slab', 'lat')), may hold values from 0 to 127
- tile_counts: int32 [8], P('slab'), may hold values from 5 to 16, as said below
- halo_blocks: int32 [8, 2, 2], P('slab'), may hold values from 0 to 3
- w_edge_in: bfloat16 [1536, 512], P(('slab', 'lat')), may hold values from -0.15625 to 0.15625
- w_edge_out: bfloat16 [512, 512], P(('slab', 'lat'))
- w_node_in: bfloat16 [1024, 512], P(('slab', 'lat')), may hold values from -0.1875 to 0.1875
- w_node_out: bfloat16 [512, 512], P(('slab', 'lat'))
- edge_gain: float32 [512], replicated, may hold values from 0.1 to 1.9
- node_gain: float32 [512], replicated, may hold values from 0.1 to 1.9
- node_cotangent: bfloat16 [4096, 512], P('slab', 'lat'), may hold values from -6 to 6
- edge_cotangent: bfloat16 [16384, 512], P(('slab', 'lat')), may hold values from -6 to 6
Outputs:
- new_nodes: bfloat16 [4096, 512], P('slab', 'lat')
- new_edges: bfloat16 [16384, 512], P(('slab', 'lat'))
- grad_nodes: bfloat16 [4096, 512], P('slab', 'lat')
- grad_edges: bfloat16 [16384, 512], P(('slab', 'lat'))
- grad_edge_in: float32 [1536, 512], P(('slab', 'lat'))
- grad_edge_out: float32 [512, 512], P(('slab', 'lat'))
- grad_node_in: float32 [1024, 512], P(('slab', 'lat'))
- grad_node_out: float32 [512, 512], P(('slab', 'lat'))
Inputs may be any that keep to these rules, and one draw needn't show every extreme that they name: `edge_tiles`: row 0 names each tile's receiver block among its slab's 4 blocks; row 1 its sender block among the 8 blocks of the extended slab (2 received from below, the slab's own, 2 received from above). Tiles of the first slab never name the blocks from below, tiles of the last slab never those from above. `tile_counts`: live tiles are the first ones of the slab's 16 slots; in every draw some slab has all slots live.
All inputs are finite; a program needn't handle non-finite values.
Results may differ from a plain program's by a relative error of at most 0.03.
The roundings to bfloat16 on the way count: a program that leaves them out, or rounds other values in their place, can miss the bound.
Values may be sent and summed in bfloat16 or wider, within the bound.
A program may use at most 64 MiB of HBM per device.

v0:
```python
import jax
import jax.numpy as jnp
from jax import lax
from jax.sharding import PartitionSpec as P

L = 512
BLK = 128
HB = 2


EPSILON = 1e-05


def from_behind(value, axis, steps):
    count = lax.axis_size(axis)
    first, last = (max(0, -steps), min(count, count - steps))
    return lax.ppermute(value, axis, [(source, source + steps) for source in range(first, last)])


def layer_norm(values, gain_vector):
    average = jnp.mean(values, axis=-1, keepdims=True)
    centred = values - average
    variance = jnp.mean(centred * centred, axis=-1, keepdims=True)
    inverse = lax.rsqrt(variance + EPSILON)
    normed = centred * inverse
    return (normed * gain_vector, normed, inverse)


def norm_back(upstream, normed, inverse, gain_vector):
    scaled = upstream * gain_vector
    return inverse * (
        scaled
        - jnp.mean(scaled, axis=-1, keepdims=True)
        - normed * jnp.mean(scaled * normed, axis=-1, keepdims=True)
    )


def contract_rows(left, right):
    return lax.dot_general(
        left, right, (((0,), (0,)), ((), ())), preferred_element_type=jnp.float32
    )


def times_transpose(left, weight):
    return lax.dot_general(
        left, weight, (((1,), (1,)), ((), ())), preferred_element_type=jnp.float32
    )


def pick_blocks(source_table, blocks):
    width = source_table.shape[1]
    return jnp.take(source_table.reshape(-1, BLK, width), blocks, axis=0).reshape(-1, width)


def add_blocks(source_table, blocks, values):
    width = source_table.shape[1]
    shaped = source_table.reshape(-1, BLK, width).at[blocks].add(values.reshape(-1, BLK, width))
    return shaped.reshape(-1, width)


def per_device(
    nodes,
    edges,
    edge_tiles,
    edge_offsets,
    tile_counts,
    halo_blocks,
    w_edge_in,
    w_edge_out,
    w_node_in,
    w_node_out,
    edge_gain,
    node_gain,
    node_cotangent,
    edge_cotangent,
):
    lat_size = lax.axis_size("lat")
    lat_index = lax.axis_index("lat")
    slab_rows = nodes.shape[0]
    own_rows = slab_rows // lat_size
    halo_rows = HB * BLK
    edge_in, edge_out, node_in, node_out = (
        lax.all_gather(w_edge_in, ("slab", "lat"), axis=0, tiled=True),
        lax.all_gather(w_edge_out, ("slab", "lat"), axis=0, tiled=True),
        lax.all_gather(w_node_in, ("slab", "lat"), axis=0, tiled=True),
        lax.all_gather(w_node_out, ("slab", "lat"), axis=0, tiled=True),
    )
    up_list = halo_blocks[0, 0]
    down_list = halo_blocks[0, 1]
    from_lower = from_behind(pick_blocks(nodes, up_list), "slab", 1)
    from_upper = from_behind(pick_blocks(nodes, down_list), "slab", -1)
    extended = lax.all_gather(
        jnp.concatenate([from_lower, nodes, from_upper], axis=0), "lat", axis=1, tiled=True
    )
    slab_full = extended[halo_rows : halo_rows + slab_rows]
    tile_slots = edge_tiles.shape[1]
    tile_of = jnp.arange(edges.shape[0], dtype=jnp.int32) // BLK
    dst_row = edge_tiles[0][tile_of] * BLK + edge_offsets[0]
    src_row = edge_tiles[1][tile_of] * BLK + edge_offsets[1]
    live_mask = (lat_index * tile_slots + tile_of < tile_counts[0]).astype(jnp.float32)[:, None]
    joined = jnp.concatenate([edges, extended[src_row], slab_full[dst_row]], axis=1)
    edge_first = jax.nn.relu(jnp.dot(joined, edge_in, preferred_element_type=jnp.float32)).astype(
        jnp.bfloat16
    )
    edge_second = jnp.dot(edge_first, edge_out, preferred_element_type=jnp.float32)
    edge_update, edge_normed, edge_inverse = layer_norm(edge_second, edge_gain)
    message = edge_update * live_mask
    new_edges = (edges.astype(jnp.float32) + message).astype(jnp.bfloat16)
    partial_sums = jnp.zeros((slab_rows, L), jnp.float32).at[dst_row].add(message)
    aggregated = lax.psum_scatter(partial_sums, "lat", scatter_dimension=0, tiled=True).astype(
        jnp.bfloat16
    )
    row_start = lat_index * own_rows
    own_latents = lax.dynamic_slice_in_dim(slab_full, row_start, own_rows, 0)
    node_joined = jnp.concatenate([own_latents, aggregated], axis=1)
    node_first = jax.nn.relu(
        jnp.dot(node_joined, node_in, preferred_element_type=jnp.float32)
    ).astype(jnp.bfloat16)
    node_second = jnp.dot(node_first, node_out, preferred_element_type=jnp.float32)
    node_update, node_normed, node_inverse = layer_norm(node_second, node_gain)
    new_rows = (own_latents.astype(jnp.float32) + node_update).astype(jnp.bfloat16)
    new_nodes = lax.all_to_all(new_rows, "lat", split_axis=1, concat_axis=0, tiled=True)
    edge_in, edge_out, node_in, node_out = (
        lax.all_gather(w_edge_in, ("slab", "lat"), axis=0, tiled=True),
        lax.all_gather(w_edge_out, ("slab", "lat"), axis=0, tiled=True),
        lax.all_gather(w_node_in, ("slab", "lat"), axis=0, tiled=True),
        lax.all_gather(w_node_out, ("slab", "lat"), axis=0, tiled=True),
    )
    node_upstream = lax.all_to_all(
        node_cotangent, "lat", split_axis=0, concat_axis=1, tiled=True
    ).astype(jnp.float32)
    d_node_second = norm_back(node_upstream, node_normed, node_inverse, node_gain).astype(
        jnp.bfloat16
    )
    g_node_out = contract_rows(node_first, d_node_second)
    d_node_first = (times_transpose(d_node_second, node_out) * (node_first > 0)).astype(
        jnp.bfloat16
    )
    g_node_in = contract_rows(node_joined, d_node_first)
    d_node_joined = times_transpose(d_node_first, node_in)
    d_direct = d_node_joined[:, :L]
    d_aggregated = d_node_joined[:, L:].astype(jnp.bfloat16)
    d_agg_slab = lax.all_gather(d_aggregated, "lat", axis=0, tiled=True)
    edge_upstream = edge_cotangent.astype(jnp.float32)
    d_message = (edge_upstream + d_agg_slab[dst_row].astype(jnp.float32)) * live_mask
    d_edge_second = norm_back(d_message, edge_normed, edge_inverse, edge_gain).astype(jnp.bfloat16)
    g_edge_out = contract_rows(edge_first, d_edge_second)
    d_edge_first = (times_transpose(d_edge_second, edge_out) * (edge_first > 0)).astype(
        jnp.bfloat16
    )
    g_edge_in = contract_rows(joined, d_edge_first)
    d_joined = times_transpose(d_edge_first, edge_in)
    grad_edges = (edge_upstream + d_joined[:, :L]).astype(jnp.bfloat16)
    d_extended = jnp.zeros((extended.shape[0], L), jnp.float32)
    d_extended = d_extended.at[src_row].add(d_joined[:, L : 2 * L])
    d_extended = d_extended.at[halo_rows + dst_row].add(d_joined[:, 2 * L :])
    own_start = halo_rows + row_start
    own_grads = lax.dynamic_slice_in_dim(d_extended, own_start, own_rows, 0) + d_direct
    d_extended = lax.dynamic_update_slice_in_dim(d_extended, own_grads, own_start, 0)
    d_narrow = lax.psum_scatter(
        d_extended.astype(jnp.bfloat16), "lat", scatter_dimension=1, tiled=True
    ).astype(jnp.float32)
    from_above = from_behind(d_narrow[:halo_rows].astype(jnp.bfloat16), "slab", -1).astype(
        jnp.float32
    )
    from_below = from_behind(
        d_narrow[halo_rows + slab_rows :].astype(jnp.bfloat16), "slab", 1
    ).astype(jnp.float32)
    grad_slab = add_blocks(
        add_blocks(d_narrow[halo_rows : halo_rows + slab_rows], up_list, from_above),
        down_list,
        from_below,
    )
    grad_nodes = grad_slab.astype(jnp.bfloat16)
    reduced_grads = (
        lax.psum_scatter(g_edge_in, ("slab", "lat"), scatter_dimension=0, tiled=True),
        lax.psum_scatter(g_edge_out, ("slab", "lat"), scatter_dimension=0, tiled=True),
        lax.psum_scatter(g_node_in, ("slab", "lat"), scatter_dimension=0, tiled=True),
        lax.psum_scatter(g_node_out, ("slab", "lat"), scatter_dimension=0, tiled=True),
    )
    return (
        new_nodes,
        new_edges,
        grad_nodes,
        grad_edges,
        reduced_grads[0],
        reduced_grads[1],
        reduced_grads[2],
        reduced_grads[3],
    )


def solution(mesh):
    placed = (
        P("slab", "lat"),
        P(("slab", "lat"), None),
        P(None, ("slab", "lat")),
        P(None, ("slab", "lat")),
        P("slab"),
        P("slab", None, None),
        P(("slab", "lat"), None),
        P(("slab", "lat"), None),
        P(("slab", "lat"), None),
        P(("slab", "lat"), None),
        P(),
        P(),
        P("slab", "lat"),
        P(("slab", "lat"), None),
    )
    return jax.shard_map(
        per_device,
        mesh=mesh,
        in_specs=placed,
        out_specs=(
            P("slab", "lat"),
            P(("slab", "lat"), None),
            P("slab", "lat"),
            P(("slab", "lat"), None),
            P(("slab", "lat"), None),
            P(("slab", "lat"), None),
            P(("slab", "lat"), None),
            P(("slab", "lat"), None),
        ),
        check_vma=False,
    )
```

profile of v0, /device:TPU:0, one launch (start us, length us, event | category | flops | bytes accessed | tf_op | source)
XLA Modules:
  0.0 814.9 jit_solution(6220979884107997981)
XLA Ops:
  7.2 0.8 compare_and_fusion.1
  8.0 1.5 gather_fusion.3
  9.5 2.3 collective-permute-start
  11.9 1.5 gather_fusion.4
  13.5 1.3 collective-permute-start.1
  14.8 3.9 collective-permute-done.1
  18.7 1.6 pad_maximum_fusion
  20.4 0.7 all-gather.6.cloned.1.call-update
  21.8 1.6 fusion.39
  23.4 5.8 compare_select_fusion
  29.3 1.1 constant_dynamic-update-slice_fusion.2
  30.4 79.1 %all_gather.24 = bf16[512,512]{1,0:T(8,128)(2,1)} all-gather(bf16[16,512]{1,0:T(8,128)(2,1)S(1)} %copy-done.21), channel_id=1, replica_groups=mesh['slab'=8,'lat'=4] {'slab','lat'}, dimensions={0}, use_global_device_ids=true | all-gather | bytes 540672 | tf_op jit(solution)/shard_map/all_gather | solution.py:84
  109.4 1.1 slice.104
  110.5 2.6 gather_fusion.1
  113.2 2.6 gather_fusion
  115.8 1.1 constant_dynamic-update-slice_fusion.1
  116.9 1.1 constant_dynamic-update-slice_fusion
  118.0 3.0 fusion.1
  121.0 1.5 fusion.40
  122.5 1.6 copy.28
  124.3 4.9 scatter_custom_fusion
  129.8 3.3 all-to-all-start.1
  133.2 72.8 %all_gather.26 = bf16[512,512]{1,0:T(8,128)(2,1)S(1)} all-gather(bf16[16,512]{1,0:T(8,128)(2,1)S(1)} %copy-done.22), channel_id=1, replica_groups=mesh['slab'=8,'lat'=4] {'slab','lat'}, dimensions={0}, use_global_device_ids=true | all-gather | bytes 540672 | tf_op jit(solution)/shard_map/all_gather | solution.py:86
  206.2 1.0 convert_element_type.82
  207.2 9.7 %all-gather.8.cloned.1.call-done = bf16[1024,512]{1,0:T(8,128)(2,1)} async-done(((bf16[32,512]{1,0:T(8,128)(2,1)}), bf16[1024,512]{1,0:T(8,128)(2,1)}) %all-gather.8.cloned.1.call-update) | async-done | bytes 1048592 | tf_op jit(solution)/shard_map/all_gather | solution.py:85
  216.9 1.6 fusion.3
  219.3 0.8 multiply_convert_fusion.1
  221.0 0.8 copy-done.10
  221.7 15.9 %all_gather.27 = bf16[512,512]{1,0:T(8,128)(2,1)S(1)} all-gather(bf16[128,512]{1,0:T(8,128)(2,1)S(1)} %slice.130), channel_id=1, replica_groups=mesh['slab'=8,'lat'=4] {'lat'}, dimensions={0}, use_global_device_ids=true | all-gather | bytes 655360 | tf_op jit(solution)/shard_map/all_gather | solution.py:143
  237.7 2.0 gather_fusion.2
  239.7 0.6 fusion.13
  240.7 1.4 multiply_convert_fusion
  242.9 0.8 copy-done.9
  243.7 1.0 fusion.43
  244.7 5.1 scatter_custom_fusion.1
  249.8 6.5 scatter_custom_fusion.2
  256.3 1.8 fusion.20
  258.1 2.7 convert_element_type.97
  260.8 2.3 copy.31
  263.1 2.7 fusion.45
  265.9 1.3 fusion.46
  267.3 4.3 fusion.44
  271.6 0.8 copy-done.14
  272.5 1.8 fusion.21
  274.4 0.9 copy-done.17
  275.2 0.7 copy.44
  275.9 3.8 all-to-all-start
  279.8 12.2 %reduce-scatter.19.cloned.1.call-done = bf16[128,1024]{1,0:T(8,128)(2,1)} async-done(((bf16[512,1024]{1,0:T(8,128)(2,1)}), bf16[128,1024]{1,0:T(8,128)(2,1)}) %reduce-scatter.19.cloned.1.call-update) | async-done | bytes 262160
  291.9 1.6 fusion.38
  293.5 1.6 copy.35
  295.0 1.6 copy.34
  296.6 1.3 collective-permute-start.2
  297.9 3.7 collective-permute-start.3
  301.6 2.0 fusion.6
  303.7 0.9 convert.13
  304.6 0.9 convert.14
  305.5 0.6 scatter_fusion
  306.1 0.6 scatter_fusion.1
  306.8 0.7 convert_element_type.98
  307.4 121.5 %reduce-scatter.13.cloned.1.call-done = f32[16,512]{1,0:T(8,128)} async-done(((f32[512,512]{1,0:T(8,128)}), f32[16,512]{1,0:T(8,128)}) %reduce-scatter.13.cloned.1.call-update) | async-done | bytes 32784 | tf_op jit(solution)/shard_map/reduce_scatter | solution.py:177
  428.9 134.9 %reduce-scatter.17.cloned.1.call-done = f32[16,512]{1,0:T(8,128)} async-done(((f32[512,512]{1,0:T(8,128)}), f32[16,512]{1,0:T(8,128)}) %reduce-scatter.17.cloned.1.call-update) | async-done | bytes 32784 | tf_op jit(solution)/shard_map/reduce_scatter | solution.py:179
  563.8 103.9 %reduce-scatter.11.cloned.1.call-done = f32[48,512]{1,0:T(8,128)} async-done(((f32[1536,512]{1,0:T(8,128)}), f32[48,512]{1,0:T(8,128)}) %reduce-scatter.11.cloned.1.call-update) | async-done | bytes 98320 | tf_op jit(solution)/shard_map/reduce_scatter | solution.py:176
  667.7 140.1 %reduce-scatter.15.cloned.1.call-done = f32[32,512]{1,0:T(8,128)} async-done(((f32[1024,512]{1,0:T(8,128)}), f32[32,512]{1,0:T(8,128)}) %reduce-scatter.15.cloned.1.call-update) | async-done | bytes 65552 | tf_op jit(solution)/shard_map/reduce_scatter | solution.py:178
  807.7 0.7 copy.53
  (98 shorter events, 4.7 us)
Async XLA Ops:
  7.2 23.2 %copy-start.21 = (bf16[16,512]{1,0:T(8,128)(2,1)S(1)}, bf16[16,512]{1,0:T(8,128)(2,1)}, u32[]{:S(2)}) copy-start(bf16[16,512]{1,0:T(8,128)(2,1)} %param.23) | copy-start | bytes 49156
  7.2 102.3 %all-gather.4.cloned.1.call-start = ((), (), s32[]{:S(2)}) async-start(), calls=%async_computation.8 | async-start | bytes 1310720 | tf_op jit(solution)/shard_map/all_gather | solution.py:92
  9.5 5.2 collective-permute-start
  13.5 5.2 collective-permute-start.1
  20.4 97.6 %all-gather.6.cloned.1.call-start = ((), (), s32[]{:S(2)}) async-start(), calls=%async_computation.9 | async-start | bytes 1622016 | tf_op jit(solution)/shard_map/all_gather | solution.py:83
  21.1 185.1 %reduce-scatter.9.cloned.1.call-start = ((), (), s32[]{:S(2)}) async-start(), calls=%async_computation.10 | async-start | bytes 1310720 | tf_op jit(solution)/shard_map/reduce_scatter | solution.py:110
  110.5 2.6 copy-start
  117.9 3.0 copy-start.1
  117.9 3.0 copy-start.3
  121.0 1.5 copy-start.5
  122.5 1.9 copy-start.20
  124.1 9.2 %copy-start.22 = (bf16[16,512]{1,0:T(8,128)(2,1)S(1)}, bf16[16,512]{1,0:T(8,128)(2,1)}, u32[]{:S(2)}) copy-start(bf16[16,512]{1,0:T(8,128)(2,1)} %param.25) | copy-start | bytes 49156
  124.3 81.7 %copy-start.19 = (f32[512]{0:T(512)S(1)}, f32[512]{0:T(512)}, u32[]{:S(2)}) copy-start(f32[512]{0:T(512)} %param.27) | copy-start | bytes 6148
  129.2 87.7 %all-gather.8.cloned.1.call-start = ((), (), s32[]{:S(2)}) async-start(), calls=%async_computation.11 | async-start | bytes 1081344 | tf_op jit(solution)/shard_map/all_gather | solution.py:85
  129.8 76.2 %all-to-all-start.1 = ((bf16[4,128,128]{2,1,0:T(8,128)(2,1)}), bf16[4,128,128]{2,1,0:T(8,128)(2,1)S(1)}, u32[]{:S(2)}, u32[]{:S(2)}) async-start(bf16[4,128,128]{2,1,0:T(8,128)(2,1)} %bitcast.20), calls=%async_computation.2 | async-start | bytes 262144 | tf_op jit(solution)/shard_map/all_to_all | solution.py:129
  133.2 158.8 %reduce-scatter.19.cloned.1.call-start = ((), (), s32[]{:S(2)}) async-start(), calls=%async_computation.16 | async-start | bytes 1310720
  206.2 13.9 %copy-start.15 = (bf16[128,512]{1,0:T(8,128)(2,1)}, bf16[128,512]{1,0:T(8,128)(2,1)S(1)}, u32[]{:S(2)}) copy-start(bf16[128,512]{1,0:T(8,128)(2,1)S(1)} %constant_dynamic-slice_fusion) | copy-start | bytes 393220
  207.2 13.2 %copy-start.13 = (bf16[128,512]{1,0:T(8,128)(2,1)}, bf16[128,512]{1,0:T(8,128)(2,1)S(1)}, u32[]{:S(2)}) copy-start(bf16[128,512]{1,0:T(8,128)(2,1)S(1)} %convert_element_type.82) | copy-start | bytes 393220
  216.9 3.5 copy-start.12
  220.9 0.8 copy-start.10
  237.7 2.0 copy-start.2
  239.6 1.0 copy-start.7
  240.2 1.9 copy-start.4
  240.2 1.9 copy-start.6
  242.1 0.8 copy-start.8
  242.1 1.6 copy-start.11
  242.9 0.8 copy-start.9
  263.1 165.8 %reduce-scatter.13.cloned.1.call-start = ((), (), s32[]{:S(2)}) async-start(), calls=%async_computation.13 | async-start | bytes 1081344 | tf_op jit(solution)/shard_map/reduce_scatter | solution.py:177
  265.8 298.0 %reduce-scatter.17.cloned.1.call-start = ((), (), s32[]{:S(2)}) async-start(), calls=%async_computation.15 | async-start | bytes 1081344 | tf_op jit(solution)/shard_map/reduce_scatter | solution.py:179
  267.2 400.4 %reduce-scatter.11.cloned.1.call-start = ((), (), s32[]{:S(2)}) async-start(), calls=%async_computation.12 | async-start | bytes 3244032 | tf_op jit(solution)/shard_map/reduce_scatter | solution.py:176
  271.6 0.9 copy-start.14
  271.6 1.0 copy-start.16
  271.6 2.8 copy-start.23
  271.6 536.1 %reduce-scatter.15.cloned.1.call-start = ((), (), s32[]{:S(2)}) async-start(), calls=%async_computation.14 | async-start | bytes 2162688 | tf_op jit(solution)/shard_map/reduce_scatter | solution.py:178
  274.3 0.9 copy-start.17
  275.9 27.6 %all-to-all-start = ((bf16[128,4,128]{2,0,1:T(8,128)(2,1)}), bf16[128,4,128]{2,0,1:T(8,128)(2,1)S(1)}, u32[]{:S(2)}, u32[]{:S(2)}) async-start(bf16[128,4,128]{2,0,1:T(8,128)(2,1)} %bitcast.87), calls=%async_computation.1 | async-start | bytes 262144 | tf_op jit(solution)/shard_map/all_to_all | solution.py:122
  291.9 11.6 %copy-start.18 = (bf16[128,1024]{1,0:T(8,128)(2,1)S(1)}, bf16[128,1024]{1,0:T(8,128)(2,1)}, u32[]{:S(2)}) copy-start(bf16[128,1024]{1,0:T(8,128)(2,1)} %reduce-scatter.19.cloned.1.call-done) | copy-start | bytes 786436
  296.6 7.1 collective-permute-start.2
  297.9 6.7 collective-permute-start.3
Sparse Core Ops, SparseCore 0:
  20.5 36.4 all-gather.3
  59.9 54.5 all-gather.5
  129.4 31.3 reduce-scatter.8
  164.0 52.8 all-gather.7
  263.2 28.6 reduce-scatter.18
  294.6 134.2 reduce-scatter.12
  431.8 131.9 reduce-scatter.16
  569.8 97.8 reduce-scatter.10
  670.5 137.1 reduce-scatter.14
where the time goes:
time: 816 us; the launch traced here: 815 us
  waiting for transfers between devices  527 us (65%)
  blocking collectives  168 us (21%)
  other arithmetic  39.6 us (5%)
  local copies, waits for them, and re-layouts  30.2 us (4%)
  matrix products  18.7 us (2%)
  starting transfers between devices  16.1 us (2%)
  between operations  15 us (2%)
    reduce_scatter x1, waiting for transfers between devices, per_device(): lax.psum_scatter(g_node_in, ('slab', 'lat'), scatter_dimension=0, tiled=T...  140 us
    reduce_scatter x1, waiting for transfers between devices, per_device(): lax.psum_scatter(g_node_out, ('slab', 'lat'), scatter_dimension=0, tiled=...  135 us
    reduce_scatter x1, waiting for transfers between devices, per_device(): lax.psum_scatter(g_edge_out, ('slab', 'lat'), scatter_dimension=0, tiled=...  121 us
    reduce_scatter x1, waiting for transfers between devices, per_device(): lax.psum_scatter(g_edge_in, ('slab', 'lat'), scatter_dimension=0, tiled=T...  104 us
    all_gather x1, blocking collectives, per_device(): lax.all_gather(w_edge_out, ('slab', 'lat'), axis=0, tiled=True)  79.1 us
    all_gather x1, blocking collectives, per_device(): lax.all_gather(w_node_out, ('slab', 'lat'), axis=0, tiled=True)  72.8 us
  transfers between devices with their start and end apart: 15, of which 7 were waited for; matrix products, arithmetic and copies ran while one was open for 5% of the time, Pallas kernels for 0%

commit v1 on v0

--- a/solution.py
+++ b/solution.py
@@ -1,6 +1,10 @@
+import functools
+
 import jax
 import jax.numpy as jnp
 from jax import lax
+from jax.experimental import pallas as pl
+from jax.experimental.pallas import tpu as pltpu
 from jax.sharding import PartitionSpec as P
 
 L = 512
@@ -9,6 +13,195 @@
 
 
 EPSILON = 1e-05
+
+MESH = pl.DeviceIdType.MESH
+GROUP_OF = (0, 1, 1, 1)
+
+
+def bits_of(count):
+    return count.bit_length() - 1
+
+
+def bit_at(index, b):
+    return lax.rem(lax.div(index, 1 << b), 2)
+
+
+def partner(axis, b):
+    index = lax.axis_index(axis)
+    return {axis: index + (1 - 2 * bit_at(index, b)) * (1 << b)}
+
+
+def greet(slab_bits, lat_bits):
+    barrier = pltpu.get_barrier_semaphore()
+    for axis, count in (("slab", slab_bits), ("lat", lat_bits)):
+        for b in range(count):
+            pl.semaphore_signal(barrier, inc=1, device_id=partner(axis, b), device_id_type=MESH)
+    pl.semaphore_wait(barrier, slab_bits + lat_bits)
+
+
+def slab_order(slab_bits, group):
+    rest = list(range(1, slab_bits))
+    return [0] + (rest if group == 0 else rest[::-1])
+
+
+def gather_kernel(slab_bits, lat_bits, *refs):
+    shards, fulls = refs[:4], refs[4:8]
+    send_sem, recv_sem = refs[8:]
+    slab, lat = lax.axis_index("slab"), lax.axis_index("lat")
+    slab_at = [bit_at(slab, b) for b in range(slab_bits)]
+    greet(slab_bits, lat_bits)
+    for shard, full in zip(shards, fulls):
+        spot = tuple(slab_at[::-1]) + (lat,)
+        full[spot] = shard[...]
+    steps = slab_bits + lat_bits
+
+    def start(i, step):
+        full = fulls[i]
+        order = slab_order(slab_bits, GROUP_OF[i])[::-1]
+        if step < lat_bits:
+            size = 1 << step
+            rows = pl.ds(lax.div(lat, size) * size, size)
+            spot = tuple(slab_at[::-1]) + (rows,)
+            to = partner("lat", step)
+        else:
+            done = order[: step - lat_bits]
+            spot = tuple(
+                slice(None) if b in done else slab_at[b] for b in reversed(range(slab_bits))
+            )
+            to = partner("slab", order[step - lat_bits])
+        copy = pltpu.make_async_remote_copy(
+            src_ref=full.at[spot],
+            dst_ref=full.at[spot],
+            send_sem=send_sem.at[i, step],
+            recv_sem=recv_sem.at[i, step],
+            device_id=to,
+            device_id_type=MESH,
+        )
+        copy.start()
+        return copy
+
+    copies = [[start(i, 0)] for i in range(4)]
+    for step in range(steps):
+        for i in range(4):
+            copies[i][step].wait_recv()
+            if step + 1 < steps:
+                copies[i].append(start(i, step + 1))
+    for row in copies:
+        for copy in row:
+            copy.wait_send()
+
+
+def gather_weights(shards, slab_count, lat_count):
+    slab_bits, lat_bits = bits_of(slab_count), bits_of(lat_count)
+    steps = slab_bits + lat_bits
+    fulls = pl.pallas_call(
+        functools.partial(gather_kernel, slab_bits, lat_bits),
+        out_shape=[
+            jax.ShapeDtypeStruct((2,) * slab_bits + (lat_count,) + w.shape, w.dtype) for w in shards
+        ],
+        in_specs=[pl.BlockSpec(memory_space=pltpu.VMEM)] * 4,
+        out_specs=[pl.BlockSpec(memory_space=pltpu.VMEM)] * 4,
+        scratch_shapes=[
+            pltpu.SemaphoreType.DMA((4, steps)),
+            pltpu.SemaphoreType.DMA((4, steps)),
+        ],
+        compiler_params=pltpu.CompilerParams(
+            collective_id=0, has_side_effects=True, vmem_limit_bytes=40 * 1024 * 1024
+        ),
+        name="gather_weights",
+    )(*shards)
+    return [full.reshape(-1, full.shape[-1]) for full in fulls]
+
+
+def sum_shapes(slab_bits, lat_count, rows, width):
+    shapes = [(2,) * (slab_bits - 1 - k) + (lat_count, rows, width) for k in range(slab_bits)]
+    while lat_count > 1:
+        lat_count //= 2
+        shapes.append((lat_count, rows, width))
+    return shapes
+
+
+def scatter_kernel(slab_bits, lat_bits, *refs):
+    steps = slab_bits + lat_bits
+    parts, outs = refs[:4], refs[4:8]
+    got = [refs[8 + i * steps : 8 + (i + 1) * steps] for i in range(4)]
+    refs = refs[8 + 4 * steps :]
+    held = [refs[i * (steps - 1) : (i + 1) * (steps - 1)] for i in range(4)]
+    send_sem, recv_sem = refs[4 * (steps - 1) :]
+    slab, lat = lax.axis_index("slab"), lax.axis_index("lat")
+    greet(slab_bits, lat_bits)
+
+    def plan(i, step):
+        if step < slab_bits:
+            order = slab_order(slab_bits, GROUP_OF[i])
+            b = order[step]
+            left = sorted(set(range(slab_bits)) - set(order[:step]), reverse=True)
+            lead = (slice(None),) * left.index(b)
+            mine = bit_at(slab, b)
+            return lead + (mine,), lead + (1 - mine,), partner("slab", b)
+        b = lat_bits - 1 - (step - slab_bits)
+        size = 1 << b
+        mine = bit_at(lat, b)
+        return (pl.ds(mine * size, size),), (pl.ds((1 - mine) * size, size),), partner("lat", b)
+
+    def source(i, step):
+        return parts[i] if step == 0 else held[i][step - 1]
+
+    def start(i, step):
+        _, theirs, to = plan(i, step)
+        copy = pltpu.make_async_remote_copy(
+            src_ref=source(i, step).at[theirs],
+            dst_ref=got[i][step],
+            send_sem=send_sem.at[i, step],
+            recv_sem=recv_sem.at[i, step],
+            device_id=to,
+            device_id_type=MESH,
+        )
+        copy.start()
+        return copy
+
+    copies = [[start(i, 0)] for i in range(4)]
+    for step in range(steps):
+        for i in range(4):
+            copies[i][step].wait_recv()
+            mine, _, _ = plan(i, step)
+            total = source(i, step)[mine].astype(jnp.float32) + got[i][step][...].astype(jnp.float32)
+            if step + 1 < steps:
+                held[i][step][...] = total.astype(jnp.bfloat16)
+                copies[i].append(start(i, step + 1))
+            else:
+                outs[i][...] = total.reshape(outs[i].shape)
+    for row in copies:
+        for copy in row:
+            copy.wait_send()
+
+
+def scatter_grads(grads, slab_count, lat_count):
+    slab_bits, lat_bits = bits_of(slab_count), bits_of(lat_count)
+    steps = slab_bits + lat_bits
+    shards = slab_count * lat_count
+    width = grads[0].shape[1]
+    shapes = [sum_shapes(slab_bits, lat_count, g.shape[0] // shards, width) for g in grads]
+    return pl.pallas_call(
+        functools.partial(scatter_kernel, slab_bits, lat_bits),
+        out_shape=[jax.ShapeDtypeStruct((g.shape[0] // shards, width), jnp.float32) for g in grads],
+        in_specs=[pl.BlockSpec(memory_space=pltpu.VMEM)] * 4,
+        out_specs=[pl.BlockSpec(memory_space=pltpu.VMEM)] * 4,
+        scratch_shapes=[pltpu.VMEM(s, jnp.bfloat16) for row in shapes for s in row]
+        + [pltpu.VMEM(s, jnp.bfloat16) for row in shapes for s in row[:-1]]
+        + [pltpu.SemaphoreType.DMA((4, steps)), pltpu.SemaphoreType.DMA((4, steps))],
+        compiler_params=pltpu.CompilerParams(
+            collective_id=1, has_side_effects=True, vmem_limit_bytes=40 * 1024 * 1024
+        ),
+        name="scatter_grads",
+    )(
+        *(
+            g.astype(jnp.bfloat16).reshape(
+                (2,) * slab_bits + (lat_count, g.shape[0] // shards, width)
+            )
+            for g in grads
+        )
+    )
 
 
 def from_behind(value, axis, steps):
@@ -79,11 +272,8 @@
     slab_rows = nodes.shape[0]
     own_rows = slab_rows // lat_size
     halo_rows = HB * BLK
-    edge_in, edge_out, node_in, node_out = (
-        lax.all_gather(w_edge_in, ("slab", "lat"), axis=0, tiled=True),
-        lax.all_gather(w_edge_out, ("slab", "lat"), axis=0, tiled=True),
-        lax.all_gather(w_node_in, ("slab", "lat"), axis=0, tiled=True),
-        lax.all_gather(w_node_out, ("slab", "lat"), axis=0, tiled=True),
+    edge_in, edge_out, node_in, node_out = gather_weights(
+        (w_edge_in, w_edge_out, w_node_in, w_node_out), lax.axis_size("slab"), lat_size
     )
     up_list = halo_blocks[0, 0]
     down_list = halo_blocks[0, 1]
@@ -120,12 +310,6 @@
     node_update, node_normed, node_inverse = layer_norm(node_second, node_gain)
     new_rows = (own_latents.astype(jnp.float32) + node_update).astype(jnp.bfloat16)
     new_nodes = lax.all_to_all(new_rows, "lat", split_axis=1, concat_axis=0, tiled=True)
-    edge_in, edge_out, node_in, node_out = (
-        lax.all_gather(w_edge_in, ("slab", "lat"), axis=0, tiled=True),
-        lax.all_gather(w_edge_out, ("slab", "lat"), axis=0, tiled=True),
-        lax.all_gather(w_node_in, ("slab", "lat"), axis=0, tiled=True),
-        lax.all_gather(w_node_out, ("slab", "lat"), axis=0, tiled=True),
-    )
     node_upstream = lax.all_to_all(
         node_cotangent, "lat", split_axis=0, concat_axis=1, tiled=True
     ).astype(jnp.float32)
@@ -172,11 +356,8 @@
         from_below,
     )
     grad_nodes = grad_slab.astype(jnp.bfloat16)
-    reduced_grads = (
-        lax.psum_scatter(g_edge_in, ("slab", "lat"), scatter_dimension=0, tiled=True),
-        lax.psum_scatter(g_edge_out, ("slab", "lat"), scatter_dimension=0, tiled=True),
-        lax.psum_scatter(g_node_in, ("slab", "lat"), scatter_dimension=0, tiled=True),
-        lax.psum_scatter(g_node_out, ("slab", "lat"), scatter_dimension=0, tiled=True),
+    reduced_grads = scatter_grads(
+        (g_edge_in, g_edge_out, g_node_in, g_node_out), lax.axis_size("slab"), lat_size
     )
     return (
         new_nodes,

time: 816 us -> 271 us (0.33)
  waiting for transfers between devices: 527 us -> 42.6 us
  blocking collectives: 168 us -> 16.1 us
  Pallas kernels: 0 us -> 82.8 us
  local copies, waits for them, and re-layouts: 30.2 us -> 44.9 us
    reduce_scatter x4 -> x0, waiting for transfers between devices: 500 us -> none  [the longest x1 140 us: per_device(): lax.psum_scatter(g_node_in, ('slab', 'lat'), scatter_dimension=0, tiled=T...]
    all_gather x2 -> x0, blocking collectives: 152 us -> none  [the longest x1 79.1 us: per_device(): lax.all_gather(w_edge_out, ('slab', 'lat'), axis=0, tiled=True)]
    pallas_call x0 -> x2, Pallas kernels: none -> 82.8 us  [the longest x1 47.4 us: gather_weights(): pl.pallas_call(functools.partial(gather_kernel, slab_bits, lat_bits), out...]
    reduce_scatter x1, waiting for transfers between devices: 0.02 us -> 12.9 us  [per_device(): lax.psum_scatter(partial_sums, 'lat', scatter_dimension=0, tiled=True)]
    all_gather x2 -> x0, waiting for transfers between devices: 9.72 us -> none  [the longest x1 9.7 us: per_device(): lax.all_gather(w_node_in, ('slab', 'lat'), axis=0, tiled=True)]
    all_to_all x1, waiting for transfers between devices: 0.01 us -> 9.68 us  [per_device(): lax.all_to_all(node_cotangent, 'lat', split_axis=0, concat_axis=1, tiled=...]
    unnamed x55 -> x69, local copies, waits for them, and re-layouts: 12.5 us -> 19 us
  transfers between devices with their start and end apart: 15 -> 9, of which waited for: 7 -> 4; matrix products, arithmetic and copies ran while one was open for 5% -> 9% of each run, Pallas kernels for 0% -> 31%
where the time goes in v1:
time: 271 us; the launch traced here: 269 us
  Pallas kernels  82.8 us (31%)
  local copies, waits for them, and re-layouts  44.9 us (17%)
  waiting for transfers between devices  42.6 us (16%)
  other arithmetic  39 us (14%)
  blocking collectives  16.1 us (6%)
  starting transfers between devices  16 us (6%)
  between operations  14.9 us (5%)
  matrix products  12.8 us (5%)
    pallas_call x1, Pallas kernels, gather_weights(): pl.pallas_call(functools.partial(gather_kernel, slab_bits, lat_bits), out...  47.4 us
    pallas_call x1, Pallas kernels, scatter_grads(): pl.pallas_call(functools.partial(scatter_kernel, slab_bits, lat_bits), ou...  35.3 us
    unnamed x69, local copies, waits for them, and re-layouts  19 us
    all_gather x1, blocking collectives, per_device(): d_agg_slab = lax.all_gather(d_aggregated, 'lat', axis=0, tiled=True)  16.1 us
    unnamed x4, waiting for transfers between devices  16 us
    reduce_scatter x1, waiting for transfers between devices, per_device(): lax.psum_scatter(partial_sums, 'lat', scatter_dimension=0, tiled=True)  12.9 us
    all_to_all x1, waiting for transfers between devices, per_device(): lax.all_to_all(node_cotangent, 'lat', split_axis=0, concat_axis=1, tiled=...  9.68 us
    ppermute x4, starting transfers between devices, from_behind(): lax.ppermute(value, axis, [(source, source + steps) for source in range(f...  8.57 us
  transfers between devices with their start and end apart: 9, of which 4 were waited for; matrix products, arithmetic and copies ran while one was open for 9% of the time, Pallas kernels for 31%

profile of v1, /device:TPU:0, one launch (start us, length us, event | category | flops | bytes accessed | tf_op | source)
XLA Modules:
  0.0 269.2 jit_solution(8425949580858597166)
XLA Ops:
  7.2 0.8 compare_and_fusion.1
  8.0 1.5 gather_fusion.3
  9.5 2.3 collective-permute-start
  11.9 1.5 gather_fusion.4
  13.5 1.3 collective-permute-start.1
  14.8 3.9 %collective-permute-done.1 = bf16[256,128]{1,0:T(8,128)(2,1)S(1)} collective-permute-done((bf16[256,128]{1,0:T(8,128)(2,1)S(1)}, bf16[256,128]{1,0:T(8,128)(2,1)S(1)}, u32[]{:S(2)}, u32[]{:S(2)}) %collective-permute-start.1) | collective-permute-done | bytes 65568 | tf_op jit(solution)/shard_map/ppermute | solution.py:210
  18.7 1.6 pad_maximum_fusion
  21.1 0.8 copy-done.3
  21.9 0.8 copy-done.4
  22.6 0.7 copy-done.5
  23.3 0.7 copy-done.6
  24.0 47.4 %gather_weights.1 = (bf16[2,2,2,4,48,512]{5,4,3,2,1,0:T(8,128)(2,1)S(1)}, bf16[2,2,2,4,16,512]{5,4,3,2,1,0:T(8,128)(2,1)S(1)}, bf16[2,2,2,4,32,512]{5,4,3,2,1,0:...) custom-call(bf16[48,512]{1,0:T(8,128)(2,1)S(1)} %copy-done.3, bf16[16,512]{1,0:T(8,128)(2,1)S(1)} %copy-done.5, ...), custom_call_target="tpu_custom_call" | custom-call | tf_op jit(solution)/shard_map/gather_weights/pallas_call | solution.py:97
  71.5 0.8 copy-done
  72.3 1.6 fusion.38
  73.8 6.0 %compare_select_fusion = (s32[512,1]{0,1:T(1,128)S(1)}, s32[512,1]{0,1:T(1,128)S(1)}, s32[512,1]{0,1:T(1,128)S(1)}) fusion(s32[2,512]{1,0:T(2,128)} %param.19, s32[]{:T(128)} %bitcast.8, s32[]{:T(128)} %bitcast.7, s32[]{:T(128)} %bitcast.6, s32[]{:T(128)} %bitcast.5, s32[]{:T(128)} %bitcast.14, s32[]{:T(128)} %bitcast.13, s32[]{:T(128)} %bitcast.12, s32[]{:T(128)} %bitcast.11), kind=kLoop, calls=%fused_computation.63 | loop fusion | flops 15872 | bytes 10272 | tf_op jit(solution)/shard_map/select_n | solution.py:340
  79.9 1.9 constant_dynamic-update-slice_fusion.2
  81.8 1.9 slice.104
  83.6 3.8 %gather_fusion.1 = bf16[512,512]{1,0:T(8,128)(2,1)} fusion(bf16[512,512]{1,0:T(8,128)(2,1)} %slice.104, s32[1024]{0:T(1024)S(1)} %pad_clamp_fusion), kind=kCustom, calls=%fused_computation.3 | custom fusion | bytes 1050624 | tf_op jit(solution)/shard_map/gather | solution.py:291
  87.4 4.0 %gather_fusion = bf16[512,512]{1,0:T(8,128)(2,1)} fusion(bf16[1024,512]{1,0:T(8,128)(2,1)} %all-gather.2.cloned.1.call-done, s32[1024]{0:T(1024)S(1)} %pad_clamp_fusion.1), kind=kCustom, calls=%fused_computation.2 | custom fusion | bytes 1050624 | tf_op jit(solution)/shard_map/gather | solution.py:291
  91.4 1.9 constant_dynamic-update-slice_fusion.1
  93.3 1.9 constant_dynamic-update-slice_fusion
  95.2 2.4 fusion.1
  97.7 1.5 fusion.39
  99.2 2.6 copy.28
  101.7 1.5 multiply_reduce_fusion.1
  103.2 5.5 %scatter_custom_fusion = f32[512,512]{1,0:T(8,128)} fusion(s32[512]{0:T(512)S(1)} %bitcast.122, f32[512,512]{1,0:T(8,128)} %copy.28, f32[512]{0:T(512)S(1)} %fusion.30, f32[512]{0:T(512)S(1)} %copy-done.27, f32[512]{0:T(512)S(1)} %add_rsqrt_fusion, f32[512]{0:T(512)S(1)} %broadcast_multiply_fusion.2, f32[]{:T(128)} %constant.70.clone.1), kind=kCustom, calls=%fused_computation.38 | custom fusion | flops 1310720 | bytes 2105348 | tf_op jit(solution)/shard_map/scatter-add | solution.py:299
  108.8 3.3 %all-to-all-start.1 = ((bf16[4,128,128]{2,1,0:T(8,128)(2,1)}), bf16[4,128,128]{2,1,0:T(8,128)(2,1)S(1)}, u32[]{:S(2)}, u32[]{:S(2)}) async-start(bf16[4,128,128]{2,1,0:T(8,128)(2,1)} %bitcast.24), calls=%async_computation.2 | async-start | bytes 262144 | tf_op jit(solution)/shard_map/all_to_all | solution.py:313
  112.2 9.7 %all-to-all-done.1 = bf16[4,128,128]{2,1,0:T(8,128)(2,1)S(1)} async-done(((bf16[4,128,128]{2,1,0:T(8,128)(2,1)}), bf16[4,128,128]{2,1,0:T(8,128)(2,1)S(1)}, u32[]{:S(2)}, u32[]{:S(2)}) %all-to-all-start.1) | async-done | bytes 131104 | tf_op jit(solution)/shard_map/all_to_all | solution.py:313
  122.0 1.6 constant_dynamic-slice_fusion
  123.6 12.9 %reduce-scatter.5.cloned.1.call-done = f32[128,512]{1,0:T(8,128)} async-done(((f32[512,512]{1,0:T(8,128)}), f32[128,512]{1,0:T(8,128)}) %reduce-scatter.5.cloned.1.call-update) | async-done | bytes 262160 | tf_op jit(solution)/shard_map/reduce_scatter | solution.py:300
  136.5 1.0 convert_element_type.94
  137.5 1.3 fusion.3
  139.5 1.7 multiply_convert_fusion.1
  141.2 0.6 copy-done.13
  142.7 0.8 copy-done.11
  143.5 16.1 %all_gather.7 = bf16[512,512]{1,0:T(8,128)(2,1)S(1)} all-gather(bf16[128,512]{1,0:T(8,128)(2,1)S(1)} %slice.130), channel_id=1, replica_groups=mesh['slab'=8,'lat'=4] {'lat'}, dimensions={0}, use_global_device_ids=true | all-gather | bytes 655360 | tf_op jit(solution)/shard_map/all_gather | solution.py:327
  159.6 2.6 gather_fusion.2
  162.2 1.9 fusion.13
  164.1 1.4 multiply_convert_fusion
  166.3 0.8 copy-done.18
  167.1 2.6 fusion.42
  169.8 4.8 %scatter_custom_fusion.1 = f32[1024,512]{1,0:T(8,128)S(1)} fusion(s32[512]{0:T(512)S(1)} %bitcast.120, f32[512,1536]{1,0:T(8,128)} %fusion.42, f32[]{:T(128)} %constant.70.clone.1), kind=kCustom, calls=%fused_computation.29 | custom fusion | flops 262144 | bytes 3146240 | tf_op jit(solution)/shard_map/scatter-add | solution.py:339
  174.6 5.1 %scatter_custom_fusion.2 = f32[1024,512]{1,0:T(8,128)S(1)} fusion(f32[1024,512]{1,0:T(8,128)S(1)} %scatter_custom_fusion.1, s32[512]{0:T(512)S(1)} %bitcast.123, f32[512,1536]{1,0:T(8,128)} %fusion.42), kind=kCustom, calls=%fused_computation.27 | custom fusion | flops 262144 | bytes 3145728 | tf_op jit(solution)/shard_map/scatter-add | solution.py:340
  179.8 1.1 convert_element_type.109
  180.9 2.4 copy.31
  183.4 0.7 copy.44
  184.0 3.9 %all-to-all-start = ((bf16[128,4,128]{2,0,1:T(8,128)(2,1)}), bf16[128,4,128]{2,0,1:T(8,128)(2,1)}, u32[]{:S(2)}, u32[]{:S(2)}) async-start(bf16[128,4,128]{2,0,1:T(8,128)(2,1)} %bitcast.95), calls=%async_computation.1 | async-start | bytes 262144 | tf_op jit(solution)/shard_map/all_to_all | solution.py:312
  188.5 1.6 convolution_convert_fusion.2
  190.2 2.2 fusion.6
  192.3 1.0 convolution_convert_fusion
  193.4 16.0 %reduce-scatter.7.cloned.1.call-done = bf16[128,1024]{1,0:T(8,128)(2,1)} async-done(((bf16[512,1024]{1,0:T(8,128)(2,1)}), bf16[128,1024]{1,0:T(8,128)(2,1)}) %reduce-scatter.7.cloned.1.call-update) | async-done | bytes 262160
  209.3 1.5 fusion.37
  210.8 1.6 copy.34
  212.4 1.3 collective-permute-start.2
  213.7 0.7 copy.35
  214.4 3.7 %collective-permute-start.3 = (bf16[256,128]{1,0:T(8,128)(2,1)}, bf16[256,128]{1,0:T(8,128)(2,1)}, u32[]{:S(2)}, u32[]{:S(2)}) collective-permute-start(bf16[256,128]{1,0:T(8,128)(2,1)} %copy.35), channel_id=1, source_target_pairs={{0,4},{4,8},{8,12},{12,16},{16,20},{20,24},{24,28},{1,5},{5,9},{9,... | collective-permute-start | bytes 196616 | tf_op jit(solution)/shard_map/ppermute | solution.py:210
  218.4 35.3 %scatter_grads.1 = (f32[48,512]{1,0:T(8,128)S(1)}, f32[16,512]{1,0:T(8,128)S(1)}, f32[32,512]{1,0:T(8,128)S(1)}, f32[16,512]{1,0:T(8,128)S(1)}) custom-call(bf16[2,2,2,4,48,512]{5,4,3,2,1,0:T(8,128)(2,1)S(1)} %bitcast.101, bf16[2,2,2,4,16,512]{5,4,3,2,1,0:T(8,128)(2,1)S(1)} %bitcast.108, bf16[2,2,2,4,32,512]{5,4,3,2,1,0:T(8,128)(2,1)S(1)} %bitcast.97, ...), custom_call_target="tpu_custom_call" | custom-call | tf_op jit(solution)/shard_map/scatter_grads/pallas_call | solution.py:185
  253.8 0.9 slice.109
  254.9 0.9 convert.13
  255.7 0.9 convert.14
  256.6 0.6 scatter_fusion
  257.2 0.6 scatter_fusion.1
  257.9 0.7 convert_element_type.110
  258.6 1.6 copy.57
  (94 shorter events, 6.3 us)
Async XLA Ops:
  7.2 74.6 %all-gather.2.cloned.1.call-start = ((), (), s32[]{:S(2)}) async-start(), calls=%async_computation.4 | async-start | bytes 1310720 | tf_op jit(solution)/shard_map/all_gather | solution.py:282
  9.5 5.2 %collective-permute-start = (bf16[256,128]{1,0:T(8,128)(2,1)S(1)}, bf16[256,128]{1,0:T(8,128)(2,1)S(1)}, u32[]{:S(2)}, u32[]{:S(2)}) collective-permute-start(bf16[256,128]{1,0:T(8,128)(2,1)S(1)} %bitcast.116), channel_id=1, source_target_pairs={{0,4},{4,8},{8,12},{12,16},{16,20},{20,24},{24,28},{1,5},{5,9},{9,... | collective-permute-start | bytes 196616 | tf_op jit(solution)/shard_map/ppermute | solution.py:210
  13.5 5.2 %collective-permute-start.1 = (bf16[256,128]{1,0:T(8,128)(2,1)S(1)}, bf16[256,128]{1,0:T(8,128)(2,1)S(1)}, u32[]{:S(2)}, u32[]{:S(2)}) collective-permute-start(bf16[256,128]{1,0:T(8,128)(2,1)S(1)} %bitcast.117), channel_id=1, source_target_pairs={{4,0},{8,4},{12,8},{16,12},{20,16},{24,20},{28,24},{5,1},{9,5},{13... | collective-permute-start | bytes 196616 | tf_op jit(solution)/shard_map/ppermute | solution.py:210
  20.3 116.2 %reduce-scatter.5.cloned.1.call-start = ((), (), s32[]{:S(2)}) async-start(), calls=%async_computation.5 | async-start | bytes 1310720 | tf_op jit(solution)/shard_map/reduce_scatter | solution.py:300
  21.0 0.8 copy-start.3
  21.9 0.8 copy-start.4
  22.6 0.7 copy-start.5
  23.3 0.7 copy-start.6
  71.5 0.8 copy-start
  95.2 2.5 copy-start.1
  97.7 1.5 copy-start.15
  99.2 4.0 %copy-start.27 = (f32[512]{0:T(512)S(1)}, f32[512]{0:T(512)}, u32[]{:S(2)}) copy-start(f32[512]{0:T(512)} %param.26) | copy-start | bytes 6148
  103.2 18.7 %copy-start.26 = (f32[512]{0:T(512)S(1)}, f32[512]{0:T(512)}, u32[]{:S(2)}) copy-start(f32[512]{0:T(512)} %param.27) | copy-start | bytes 6148
  108.8 13.1 %all-to-all-start.1 = ((bf16[4,128,128]{2,1,0:T(8,128)(2,1)}), bf16[4,128,128]{2,1,0:T(8,128)(2,1)S(1)}, u32[]{:S(2)}, u32[]{:S(2)}) async-start(bf16[4,128,128]{2,1,0:T(8,128)(2,1)} %bitcast.24), calls=%async_computation.2 | async-start | bytes 262144 | tf_op jit(solution)/shard_map/all_to_all | solution.py:313
  112.1 97.2 %reduce-scatter.7.cloned.1.call-start = ((), (), s32[]{:S(2)}) async-start(), calls=%async_computation.6 | async-start | bytes 1310720
  137.5 1.3 copy-start.22
  141.2 0.6 copy-start.13
  142.7 0.8 copy-start.11
  159.6 2.6 copy-start.7
  162.2 1.9 copy-start.8
  162.2 1.9 copy-start.9
  162.2 1.9 copy-start.10
  164.1 1.4 copy-start.2
  164.1 1.4 copy-start.16
  165.6 0.8 copy-start.21
  166.3 0.8 copy-start.18
  174.6 5.1 %copy-start.12 = (f32[128,1024]{1,0:T(8,128)S(1)}, f32[128,1024]{1,0:T(8,128)}, u32[]{:S(2)}) copy-start(f32[128,1024]{1,0:T(8,128)} %copy-done.11) | copy-start | bytes 1572868
  180.9 2.4 copy-start.28
  180.9 2.4 copy-start.20
  180.9 7.1 %copy-start.23 = (bf16[128,512]{1,0:T(8,128)(2,1)S(1)}, bf16[128,512]{1,0:T(8,128)(2,1)}, u32[]{:S(2)}) copy-start(bf16[128,512]{1,0:T(8,128)(2,1)} %copy-done.22) | copy-start | bytes 393220
  180.9 7.1 %copy-start.24 = (bf16[128,512]{1,0:T(8,128)(2,1)S(1)}, bf16[128,512]{1,0:T(8,128)(2,1)}, u32[]{:S(2)}) copy-start(bf16[128,512]{1,0:T(8,128)(2,1)} %constant_dynamic-slice_fusion) | copy-start | bytes 393220
  183.3 5.2 %copy-start.17 = (bf16[512,512]{1,0:T(8,128)(2,1)S(1)}, bf16[512,512]{1,0:T(8,128)(2,1)}, u32[]{:S(2)}) copy-start(bf16[512,512]{1,0:T(8,128)(2,1)} %copy-done.15) | copy-start | bytes 1572868
  184.0 69.7 %all-to-all-start = ((bf16[128,4,128]{2,0,1:T(8,128)(2,1)}), bf16[128,4,128]{2,0,1:T(8,128)(2,1)}, u32[]{:S(2)}, u32[]{:S(2)}) async-start(bf16[128,4,128]{2,0,1:T(8,128)(2,1)} %bitcast.95), calls=%async_computation.1 | async-start | bytes 262144 | tf_op jit(solution)/shard_map/all_to_all | solution.py:312
  188.5 3.9 %copy-start.19 = (bf16[512,512]{1,0:T(8,128)(2,1)S(1)}, bf16[512,512]{1,0:T(8,128)(2,1)}, u32[]{:S(2)}) copy-start(bf16[512,512]{1,0:T(8,128)(2,1)} %copy-done.18) | copy-start | bytes 1572868
  188.5 3.9 %copy-start.25 = (bf16[512,1536]{1,0:T(8,128)(2,1)S(1)}, bf16[512,1536]{1,0:T(8,128)(2,1)}, u32[]{:S(2)}) copy-start(bf16[512,1536]{1,0:T(8,128)(2,1)} %constant_dynamic-update-slice_fusion) | copy-start | bytes 4718596
  192.3 25.8 %copy-start.14 = (bf16[128,512]{1,0:T(8,128)(2,1)S(1)}, bf16[128,512]{1,0:T(8,128)(2,1)}, u32[]{:S(2)}) copy-start(bf16[128,512]{1,0:T(8,128)(2,1)} %copy-done.13) | copy-start | bytes 393220
  212.4 42.4 %collective-permute-start.2 = (bf16[256,128]{1,0:T(8,128)(2,1)}, bf16[256,128]{1,0:T(8,128)(2,1)}, u32[]{:S(2)}, u32[]{:S(2)}) collective-permute-start(bf16[256,128]{1,0:T(8,128)(2,1)} %copy.34), channel_id=1, source_target_pairs={{4,0},{8,4},{12,8},{16,12},{20,16},{24,20},{28,24},{5,1},{9,5},{13... | collective-permute-start | bytes 196616 | tf_op jit(solution)/shard_map/ppermute | solution.py:210
  214.4 41.3 %collective-permute-start.3 = (bf16[256,128]{1,0:T(8,128)(2,1)}, bf16[256,128]{1,0:T(8,128)(2,1)}, u32[]{:S(2)}, u32[]{:S(2)}) collective-permute-start(bf16[256,128]{1,0:T(8,128)(2,1)} %copy.35), channel_id=1, source_target_pairs={{0,4},{4,8},{8,12},{12,16},{16,20},{20,24},{24,28},{1,5},{5,9},{9,... | collective-permute-start | bytes 196616 | tf_op jit(solution)/shard_map/ppermute | solution.py:210
Sparse Core Ops, SparseCore 0:
  20.5 42.3 all-gather.1
  108.9 27.5 reduce-scatter.4
  183.5 25.8 reduce-scatter.6

commit v2 on v0

v2 whole, which is shorter than its diff:
```python
import functools
import itertools
import types

import jax
import jax.numpy as jnp
from jax import lax
from jax.experimental import pallas as pl
from jax.experimental.pallas import tpu as pltpu
from jax.sharding import PartitionSpec as P

L = 512
BLK = 128
HB = 2


EPSILON = 1e-05

MESH = pl.DeviceIdType.MESH
GROUP_OF = (0, 1, 0, 1)


def pieces_of(rows, group):
    head = rows * 2 // 3 // 16 * 16
    if rows % 16 or not 0 < head < rows or group:
        return [(0, rows, group)]
    return [(0, head, 0), (head, rows - head, 1)] if rows >= 48 else [(0, rows, group)]


def bits_of(count):
    return count.bit_length() - 1


def bit_at(index, b):
    return lax.rem(lax.div(index, 1 << b), 2)


def partner(axis, b):
    index = lax.axis_index(axis)
    return {axis: index + (1 - 2 * bit_at(index, b)) * (1 << b)}


def layer_norm(values, gain_vector):
    average = jnp.mean(values, axis=-1, keepdims=True)
    centred = values - average
    variance = jnp.mean(centred * centred, axis=-1, keepdims=True)
    inverse = lax.rsqrt(variance + EPSILON)
    normed = centred * inverse
    return (normed * gain_vector, normed, inverse)


def norm_back(upstream, normed, inverse, gain_vector):
    scaled = upstream * gain_vector
    return inverse * (
        scaled
        - jnp.mean(scaled, axis=-1, keepdims=True)
        - normed * jnp.mean(scaled * normed, axis=-1, keepdims=True)
    )


def contract_rows(left, right):
    return lax.dot_general(
        left, right, (((0,), (0,)), ((), ())), preferred_element_type=jnp.float32
    )


def times_transpose(left, weight):
    return lax.dot_general(
        left, weight, (((1,), (1,)), ((), ())), preferred_element_type=jnp.float32
    )


def slab_order(slab_bits, group):
    rest = list(range(1, slab_bits))
    return [0] + (rest if group == 0 else rest[::-1])


def dot(left, right):
    return jnp.dot(left, right, preferred_element_type=jnp.float32)


def sum_shapes(slab_bits, lat_count, rows, width):
    shapes = [(2,) * (slab_bits - 1 - k) + (lat_count, rows, width) for k in range(slab_bits)]
    while lat_count > 1:
        lat_count //= 2
        shapes.append((lat_count, rows, width))
    return shapes


def spots_of(slab_bits, lat_count):
    return list(itertools.product(*([range(2)] * slab_bits + [range(lat_count)])))


def layer_kernel(slab_bits, lat_bits, names, *refs):
    r = types.SimpleNamespace()
    for name, ref in zip(names, refs):
        if isinstance(name, str):
            setattr(r, name, ref)
        else:
            vars(r).setdefault(name[0], []).append(ref)
    r.got = [r.got[n : n + slab_bits + lat_bits] for n in range(0, len(r.got), slab_bits + lat_bits)]
    held_steps = slab_bits + lat_bits - 1
    r.held = [r.held[n : n + held_steps] for n in range(0, len(r.held), held_steps)]
    slab_count, lat_count = 1 << slab_bits, 1 << lat_bits
    steps = slab_bits + lat_bits
    slab, lat = lax.axis_index("slab"), lax.axis_index("lat")
    slab_at = [bit_at(slab, b) for b in range(slab_bits)]
    send_sem, recv_sem = r.send_sem, r.recv_sem
    slab_rows, width = r.nodes.shape
    own_rows = slab_rows // lat_count
    halo_rows = HB * BLK
    all_rows = slab_rows + 2 * halo_rows
    edge_rows = r.edges.shape[0]
    tiles = edge_rows // BLK
    bf16, f32 = jnp.bfloat16, jnp.float32
    has_lower, has_upper = slab > 0, slab < slab_count - 1
    lower, upper = {"slab": slab - 1}, {"slab": slab + 1}
    sems = itertools.count()
    sent = []

    def remote(source, target, to):
        k = next(sems)
        return pltpu.make_async_remote_copy(
            src_ref=source,
            dst_ref=target,
            send_sem=send_sem.at[k],
            recv_sem=recv_sem.at[k],
            device_id=to,
            device_id_type=MESH,
        )

    def begin(copy):
        copy.start()
        sent.append(copy)
        return copy

    def peer(k):
        return lax.rem(lat + k, lat_count)

    barrier = pltpu.get_barrier_semaphore()
    for b in range(slab_bits):
        pl.semaphore_signal(barrier, inc=1, device_id=partner("slab", b), device_id_type=MESH)
    for k in range(1, lat_count):
        pl.semaphore_signal(barrier, inc=1, device_id={"lat": peer(k)}, device_id_type=MESH)

    @pl.when(has_lower)
    def _():
        pl.semaphore_signal(barrier, inc=1, device_id=lower, device_id_type=MESH)

    @pl.when(has_upper)
    def _():
        pl.semaphore_signal(barrier, inc=1, device_id=upper, device_id_type=MESH)

    pl.semaphore_wait(
        barrier, slab_bits + lat_count - 1 + has_lower.astype(jnp.int32) + has_upper.astype(jnp.int32)
    )

    shards = [r.w0, r.w1, r.w2, r.w3]
    pieces = [(i, *p) for i in range(4) for p in pieces_of(shards[i].shape[0], GROUP_OF[i])]
    count = len(pieces)
    fulls = r.full
    for (i, start, rows, _), full in zip(pieces, fulls):
        full[tuple(slab_at[::-1]) + (lat,)] = shards[i][start : start + rows, :]

    def gather_start(p, step):
        full = fulls[p]
        order = slab_order(slab_bits, pieces[p][3])[::-1]
        if step < lat_bits:
            size = 1 << step
            spot = tuple(slab_at[::-1]) + (pl.ds(lax.div(lat, size) * size, size),)
            to = partner("lat", step)
        else:
            done = order[: step - lat_bits]
            spot = tuple(
                slice(None) if b in done else slab_at[b] for b in reversed(range(slab_bits))
            )
            to = partner("slab", order[step - lat_bits])
        gathers[p].append(begin(remote(full.at[spot], full.at[spot], to)))

    gathers = [[] for _ in pieces]
    edge_pieces = [p for p in range(count) if pieces[p][0] < 2]
    node_pieces = [p for p in range(count) if pieces[p][0] >= 2]

    def gather_step(which, step):
        for p in which:
            if step >= 0:
                gathers[p][step].wait_recv()
            if step + 1 < steps:
                gather_start(p, step + 1)

    gather_step(edge_pieces, -1)

    def whole(i):
        mine = [fulls[p] for p in range(count) if pieces[p][0] == i]
        rows, cols = shards[i].shape
        total = rows << steps
        if rows % 16 == 0:
            blocks = [full[...].reshape(-1, full.shape[-2], cols) for full in mine]
            return jnp.concatenate(blocks, axis=1).reshape(total, cols)
        full, wide = mine[0], r.wide
        for n, spot in enumerate(spots_of(slab_bits, lat_count)):
            wide[n * rows : (n + 1) * rows, :] = full[spot].astype(f32)
        return wide[0:total, :].astype(bf16)

    own, low, up, cot = r.own, r.low, r.up, r.cot
    own[lat] = r.nodes[...]
    own_copies, cot_copies = [], []
    for k in range(1, lat_count):
        own_copies.append(begin(remote(r.nodes, own.at[lat], {"lat": peer(k)})))

    def places(which, count):
        pieces = [
            r.edge_offsets[which : which + 1, t * BLK : (t + 1) * BLK]
            + r.edge_tiles[which, t] * BLK
            for t in range(tiles)
        ]
        row = jnp.concatenate(pieces, axis=1)
        cells = lax.broadcasted_iota(jnp.int32, (count, edge_rows), 0)
        return jnp.where(cells == row, 1.0, 0.0).astype(bf16)

    r.recv_hot[...] = places(0, slab_rows)
    r.send_hot[...] = places(1, all_rows)
    chunk = 2 * BLK
    parts = edge_rows // chunk

    def rows_of(n):
        return pl.ds(pl.multiple_of(n * chunk, chunk), chunk)

    def live_of(n):
        tile = lat * tiles + (
            n * chunk + lax.broadcasted_iota(jnp.int32, (chunk, 1), 0)
        ) // BLK
        return jnp.where(tile < r.tile_counts[0], 1.0, 0.0).astype(f32)

    gather_step(edge_pieces, 0)
    for copy in own_copies:
        copy.wait_recv()
    for side, staged in ((0, r.to_upper), (1, r.to_lower)):
        for j in range(HB):
            picked = jnp.zeros((lat_count, BLK, width), f32)
            for block in range(slab_rows // BLK):
                hit = (r.halo_blocks[0, side, j] == block).astype(f32)
                picked = picked + hit * own[:, block * BLK : (block + 1) * BLK, :].astype(f32)
            staged[:, j * BLK : (j + 1) * BLK, :] = picked.astype(bf16)

    def halo_exchange(to_upper, to_lower, low_place, up_place):
        upward = remote(to_upper, low_place, upper)
        downward = remote(to_lower, up_place, lower)

        @pl.when(has_upper)
        def _():
            upward.start()

        @pl.when(has_lower)
        def _():
            downward.start()

        def arrive():
            @pl.when(has_lower)
            def _():
                upward.wait_recv()

            @pl.when(jnp.logical_not(has_lower))
            def _():
                low_place[...] = jnp.zeros(low_place.shape, low_place.dtype)

            @pl.when(has_upper)
            def _():
                downward.wait_recv()

            @pl.when(jnp.logical_not(has_upper))
            def _():
                up_place[...] = jnp.zeros(up_place.shape, up_place.dtype)

        def leave():
            @pl.when(has_upper)
            def _():
                upward.wait_send()

            @pl.when(has_lower)
            def _():
                downward.wait_send()

        return arrive, leave

    arrive, leave_latents = halo_exchange(r.to_upper, r.to_lower, low, up)
    for step in range(1, steps - 1):
        gather_step(edge_pieces, step)
        gather_step(node_pieces, step - 2)
    arrive()
    ext = r.ext
    for t in range(lat_count):
        cols = slice(t * width, (t + 1) * width)
        ext[0:halo_rows, cols] = low[t]
        ext[halo_rows : halo_rows + slab_rows, cols] = own[t]
        ext[halo_rows + slab_rows :, cols] = up[t]
    joined = r.joined
    joined[0] = r.edges[...]
    joined[1] = contract_rows(r.send_hot[...], ext[...]).astype(bf16)
    joined[2] = contract_rows(
        r.recv_hot[...], ext[halo_rows : halo_rows + slab_rows, :]
    ).astype(bf16)
    gather_step(edge_pieces, steps - 1)
    gather_step(node_pieces, steps - 3)
    edge_in, edge_out, node_in, node_out = r.mat0, r.mat1, r.mat2, r.mat3
    edge_in[...], edge_out[...] = whole(0), whole(1)
    edge_gain, node_gain = r.edge_gain[...], r.node_gain[...]

    def edge_forward(n, carry):
        rows = rows_of(n)
        first = dot(joined[0, rows, :], edge_in[0:L, :])
        first += dot(joined[1, rows, :], edge_in[L : 2 * L, :])
        first += dot(joined[2, rows, :], edge_in[2 * L :, :])
        first = jnp.maximum(first, 0.0).astype(bf16)
        r.first[rows, :] = first
        update, normed, inverse = layer_norm(dot(first, edge_out[...]), edge_gain)
        r.normed[rows, :] = normed
        r.inverse[rows, :] = inverse
        message = update * live_of(n)
        r.new_edges[rows, :] = (r.edges[rows, :].astype(f32) + message).astype(bf16)
        top = message.astype(bf16)
        r.top[rows, :] = top
        r.rest[rows, :] = (message - top.astype(f32)).astype(bf16)
        return carry

    half = parts // 2
    lax.fori_loop(0, half, edge_forward, 0)
    gather_step(node_pieces, steps - 2)
    lax.fori_loop(half, parts, edge_forward, 0)
    sums = dot(r.recv_hot[...], r.top[...]) + dot(r.recv_hot[...], r.rest[...])
    r.sums[...] = sums.reshape(lat_count, own_rows, L)
    sum_copies = [
        begin(remote(r.sums.at[peer(k)], r.sums_got.at[k - 1], {"lat": peer(k)}))
        for k in range(1, lat_count)
    ]
    for k in range(1, lat_count):
        rows = pl.ds(pl.multiple_of(peer(k) * own_rows, own_rows), own_rows)
        cot_copies.append(
            begin(remote(r.node_cotangent.at[rows], cot.at[lat], {"lat": peer(k)}))
        )
    cot[lat] = r.node_cotangent[pl.ds(pl.multiple_of(lat * own_rows, own_rows), own_rows), :]
    gather_step(node_pieces, steps - 1)
    node_in[...], node_out[...] = whole(2), whole(3)
    own_latents = ext[pl.ds(pl.multiple_of(halo_rows + lat * own_rows, own_rows), own_rows), :]
    for copy in cot_copies:
        copy.wait_recv()
    upstream = jnp.concatenate([cot[t] for t in range(lat_count)], axis=1).astype(f32)
    node_pre = dot(own_latents, node_in[0:L, :])
    total = r.sums[lat]
    for k, copy in enumerate(sum_copies):
        copy.wait_recv()
        total = total + r.sums_got[k]
    aggregated = total.astype(bf16)

    node_first = jnp.maximum(node_pre + dot(aggregated, node_in[L:, :]), 0.0).astype(bf16)
    update, normed, inverse = layer_norm(dot(node_first, node_out[...]), node_gain)
    new_rows = (own_latents.astype(f32) + update).astype(bf16)
    d_second = norm_back(upstream, normed, inverse, node_gain).astype(bf16)
    d_first = (times_transpose(d_second, node_out[...]) * (node_first > 0).astype(f32)).astype(bf16)
    d_agg = r.d_agg
    d_agg[lat] = times_transpose(d_first, node_in[L:, :]).astype(bf16)
    agg_copies = [
        begin(remote(d_agg.at[lat], d_agg.at[lat], {"lat": peer(k)})) for k in range(1, lat_count)
    ]
    for t in range(lat_count):
        r.rows_out[t] = new_rows[:, t * width : (t + 1) * width]
    r.new_nodes[lat] = r.rows_out[lat]
    out_copies = [
        begin(remote(r.rows_out.at[peer(k)], r.new_nodes.at[lat], {"lat": peer(k)}))
        for k in range(1, lat_count)
    ]

    sum_refs, got, held = r.grad, r.got, r.held
    grad_outs = [r.grad_out0, r.grad_out1, r.grad_out2, r.grad_out3]
    scatters = [[] for _ in pieces]

    def scatter_plan(i, step):
        if step < slab_bits:
            order = slab_order(slab_bits, pieces[i][3])
            b = order[step]
            left = sorted(set(range(slab_bits)) - set(order[:step]), reverse=True)
            lead = (slice(None),) * left.index(b)
            return lead + (slab_at[b],), lead + (1 - slab_at[b],), partner("slab", b)
        b = lat_bits - 1 - (step - slab_bits)
        size = 1 << b
        mine = bit_at(lat, b)
        return (pl.ds(mine * size, size),), (pl.ds((1 - mine) * size, size),), partner("lat", b)

    def scatter_source(i, step):
        return sum_refs[i] if step == 0 else held[i][step - 1]

    def scatter_start(i, step):
        _, theirs, to = scatter_plan(i, step)
        scatters[i].append(
            begin(remote(scatter_source(i, step).at[theirs], got[i][step], to))
        )

    def scatter_step(i, step):
        scatters[i][step].wait_recv()
        mine, _, _ = scatter_plan(i, step)
        total = scatter_source(i, step)[mine].astype(f32) + got[i][step][...].astype(f32)
        if step + 1 < steps:
            held[i][step][...] = total.astype(bf16)
            scatter_start(i, step + 1)
        else:
            k, start, rows, _ = pieces[i]
            grad_outs[k][start : start + rows, :] = total.reshape(rows, total.shape[-1])

    def put_grad(i, values):
        rows = shards[i].shape[0]
        mine = [p for p in range(count) if pieces[p][0] == i]
        if rows % 16 == 0:
            cut = values.astype(bf16).reshape(-1, rows, values.shape[1])
            for p in mine:
                _, start, some, _ = pieces[p]
                sum_refs[p][...] = cut[:, start : start + some, :].reshape(sum_refs[p].shape)
        else:
            wide = r.wide
            wide[0 : values.shape[0], :] = values
            for n, spot in enumerate(spots_of(slab_bits, lat_count)):
                sum_refs[mine[0]][spot] = wide[n * rows : (n + 1) * rows, :].astype(bf16)
        for p in mine:
            scatter_start(p, 0)

    put_grad(3, contract_rows(node_first, d_second))
    put_grad(
        2, contract_rows(jnp.concatenate([own_latents, aggregated], axis=1), d_first)
    )
    d_direct = times_transpose(d_first, node_in[0:L, :])
    for p in node_pieces:
        scatter_step(p, 0)

    for copy in agg_copies:
        copy.wait_recv()
    r.d_edge[...] = contract_rows(
        r.recv_hot[...], d_agg[...].reshape(slab_rows, L)
    ).astype(bf16)

    def edge_second(n, carry):
        rows = rows_of(n)
        d_message = (
            r.edge_cotangent[rows, :].astype(f32) + r.d_edge[rows, :].astype(f32)
        ) * live_of(n)
        d_second = norm_back(d_message, r.normed[rows, :], r.inverse[rows, :], edge_gain)
        r.top[rows, :] = d_second.astype(bf16)
        return carry

    lax.fori_loop(0, parts, edge_second, 0)
    put_grad(1, contract_rows(r.first[...], r.top[...]))
    for p in node_pieces:
        scatter_step(p, 1)

    def edge_first(n, carry):
        rows = rows_of(n)
        d_first = times_transpose(r.top[rows, :], edge_out[...])
        r.rest[rows, :] = (d_first * (r.first[rows, :] > 0).astype(f32)).astype(bf16)
        return carry

    lax.fori_loop(0, parts, edge_first, 0)
    def edge_joined(n, carry):
        rows = rows_of(n)
        d_first = r.rest[rows, :]
        direct = times_transpose(d_first, edge_in[0:L, :])
        r.grad_edges[rows, :] = (
            r.edge_cotangent[rows, :].astype(f32) + direct
        ).astype(bf16)
        r.far[rows, :] = times_transpose(d_first, edge_in[L : 2 * L, :]).astype(bf16)
        r.d_edge[rows, :] = times_transpose(d_first, edge_in[2 * L :, :]).astype(bf16)
        return carry

    lax.fori_loop(0, parts, edge_joined, 0)
    d_ext = r.d_ext
    d_ext[...] = dot(r.send_hot[...], r.far[...])
    d_ext[halo_rows : halo_rows + slab_rows, :] += dot(r.recv_hot[...], r.d_edge[...])
    mine = pl.ds(pl.multiple_of(halo_rows + lat * own_rows, own_rows), own_rows)
    d_ext[mine, :] += d_direct
    r.back_low[...] = d_ext[0:halo_rows, :].astype(bf16)
    r.back_up[...] = d_ext[halo_rows + slab_rows :, :].astype(bf16)
    arrive, leave_grads = halo_exchange(
        r.back_up, r.back_low, r.from_below, r.from_above
    )
    put_grad(
        0,
        jnp.concatenate([contract_rows(joined[k], r.rest[...]) for k in range(3)], axis=0),
    )
    arrive()
    for block in range(slab_rows // BLK):
        rows = slice(halo_rows + block * BLK, halo_rows + (block + 1) * BLK)
        total = d_ext[rows, :]
        for side, place in ((0, r.from_above), (1, r.from_below)):
            for j in range(HB):
                hit = (r.halo_blocks[0, side, j] == block).astype(f32)
                total = total + hit * place[j * BLK : (j + 1) * BLK, :].astype(f32)
        total = total.astype(bf16)
        for t in range(lat_count):
            r.d_cut[t, block * BLK : (block + 1) * BLK, :] = total[
                :, t * width : (t + 1) * width
            ]
    cut_copies = [
        begin(remote(r.d_cut.at[peer(k)], r.d_got.at[k - 1], {"lat": peer(k)}))
        for k in range(1, lat_count)
    ]
    for step in range(steps):
        for p in node_pieces:
            if step + 2 < steps:
                scatter_step(p, step + 2)
        for p in edge_pieces[::-1]:
            scatter_step(p, step)
    narrow = r.d_cut[lat].astype(f32)
    for k, copy in enumerate(cut_copies):
        copy.wait_recv()
        narrow = narrow + r.d_got[k].astype(f32)
    r.grad_nodes[...] = narrow.astype(bf16)
    for copy in out_copies:
        copy.wait_recv()
    for copy in sent:
        copy.wait_send()
    leave_latents()
    leave_grads()


def per_device(
    nodes,
    edges,
    edge_tiles,
    edge_offsets,
    tile_counts,
    halo_blocks,
    w_edge_in,
    w_edge_out,
    w_node_in,
    w_node_out,
    edge_gain,
    node_gain,
    node_cotangent,
    edge_cotangent,
):
    slab_count, lat_count = lax.axis_size("slab"), lax.axis_size("lat")
    slab_bits, lat_bits = bits_of(slab_count), bits_of(lat_count)
    steps = slab_bits + lat_bits
    slab_rows, width = nodes.shape
    own_rows = slab_rows // lat_count
    halo_rows = HB * BLK
    all_rows = slab_rows + 2 * halo_rows
    edge_rows = edges.shape[0]
    bf16, f32 = jnp.bfloat16, jnp.float32
    weights = (w_edge_in, w_edge_out, w_node_in, w_node_out)
    whole_rows = [w.shape[0] * slab_count * lat_count for w in weights]
    vmem, smem = pl.BlockSpec(memory_space=pltpu.VMEM), pl.BlockSpec(memory_space=pltpu.SMEM)
    inputs = dict(
        nodes=nodes,
        edges=edges,
        edge_tiles=edge_tiles,
        edge_offsets=edge_offsets,
        tile_counts=tile_counts,
        halo_blocks=halo_blocks,
        w0=w_edge_in,
        w1=w_edge_out,
        w2=w_node_in,
        w3=w_node_out,
        edge_gain=edge_gain.reshape(1, -1),
        node_gain=node_gain.reshape(1, -1),
        node_cotangent=node_cotangent,
        edge_cotangent=edge_cotangent,
    )
    outputs = dict(
        new_nodes=((lat_count, own_rows, width), bf16),
        new_edges=(edges.shape, bf16),
        grad_nodes=(nodes.shape, bf16),
        grad_edges=(edges.shape, bf16),
        grad_out0=(w_edge_in.shape, f32),
        grad_out1=(w_edge_out.shape, f32),
        grad_out2=(w_node_in.shape, f32),
        grad_out3=(w_node_out.shape, f32),
    )
    scratch = dict(
        own=((lat_count, slab_rows, width), bf16),
        low=((lat_count, halo_rows, width), bf16),
        up=((lat_count, halo_rows, width), bf16),
        to_upper=((lat_count, halo_rows, width), bf16),
        to_lower=((lat_count, halo_rows, width), bf16),
        cot=((lat_count, own_rows, width), bf16),
        recv_hot=((slab_rows, edge_rows), bf16),
        send_hot=((all_rows, edge_rows), bf16),
        ext=((all_rows, L), bf16),
        joined=((3, edge_rows, L), bf16),
        first=((edge_rows, L), bf16),
        normed=((edge_rows, L), f32),
        inverse=((edge_rows, 1), f32),
        top=((edge_rows, L), bf16),
        rest=((edge_rows, L), bf16),
        sums=((lat_count, own_rows, L), f32),
        sums_got=((lat_count - 1, own_rows, L), f32),
        d_agg=((lat_count, own_rows, L), bf16),
        rows_out=((lat_count, own_rows, width), bf16),
        d_edge=((edge_rows, L), bf16),
        d_ext=((all_rows, L), f32),
        d_cut=((lat_count, slab_rows, width), bf16),
        d_got=((lat_count - 1, slab_rows, width), bf16),
        back_low=((halo_rows, L), bf16),
        back_up=((halo_rows, L), bf16),
        from_below=((halo_rows, L), bf16),
        from_above=((halo_rows, L), bf16),
        far=((edge_rows, L), bf16),
        mat0=((whole_rows[0], L), bf16),
        mat1=((whole_rows[1], L), bf16),
        mat2=((whole_rows[2], L), bf16),
        mat3=((whole_rows[3], L), bf16),
        wide=((max(whole_rows), L), f32),
    )
    names, shapes = list(scratch), list(scratch.values())
    for i in range(4):
        for _, rows, _ in pieces_of(weights[i].shape[0], GROUP_OF[i]):
            cut = (2,) * slab_bits + (lat_count, rows, L)
            names += [("full",), ("grad",)]
            shapes += [(cut, bf16)] * 2
            for k, shape in enumerate(sum_shapes(slab_bits, lat_count, rows, L)):
                names.append(("got",))
                shapes.append((shape, bf16))
                if k + 1 < steps:
                    names.append(("held",))
                    shapes.append((shape, bf16))
    count = names.count(("full",))
    copies = 2 * count * steps + 6 * (lat_count - 1) + 4
    results = pl.pallas_call(
        functools.partial(
            layer_kernel,
            slab_bits,
            lat_bits,
            [*inputs, *outputs, *names, "send_sem", "recv_sem"],
        ),
        out_shape=[jax.ShapeDtypeStruct(*o) for o in outputs.values()],
        in_specs=[smem if n in (2, 4, 5) else vmem for n in range(len(inputs))],
        out_specs=[vmem] * len(outputs),
        scratch_shapes=[pltpu.VMEM(*s) for s in shapes]
        + [pltpu.SemaphoreType.DMA((copies,)), pltpu.SemaphoreType.DMA((copies,))],
        compiler_params=pltpu.CompilerParams(
            collective_id=0, has_side_effects=True, vmem_limit_bytes=56 * 1024 * 1024
        ),
        name="mesh_layer",
    )(*inputs.values())
    return (results[0].reshape(nodes.shape), *results[1:])


def solution(mesh):
    placed = (
        P("slab", "lat"),
        P(("slab", "lat"), None),
        P(None, ("slab", "lat")),
        P(None, ("slab", "lat")),
        P("slab"),
        P("slab", None, None),
        P(("slab", "lat"), None),
        P(("slab", "lat"), None),
        P(("slab", "lat"), None),
        P(("slab", "lat"), None),
        P(),
        P(),
        P("slab", "lat"),
        P(("slab", "lat"), None),
    )
    return jax.shard_map(
        per_device,
        mesh=mesh,
        in_specs=placed,
        out_specs=(
            P("slab", "lat"),
            P(("slab", "lat"), None),
            P("slab", "lat"),
            P(("slab", "lat"), None),
            P(("slab", "lat"), None),
            P(("slab", "lat"), None),
            P(("slab", "lat"), None),
            P(("slab", "lat"), None),
        ),
        check_vma=False,
    )
```

time: 816 us -> 139 us (0.17)
  waiting for transfers between devices: 527 us -> 0 us
  blocking collectives: 168 us -> 0 us
  Pallas kernels: 0 us -> 129 us
  other arithmetic: 39.6 us -> 0 us
  local copies, waits for them, and re-layouts: 30.2 us -> 8.11 us
  matrix products: 18.7 us -> 0 us
  starting transfers between devices: 16.1 us -> 0 us
  between operations: 15 us -> 1.3 us
    reduce_scatter x5 -> x0, waiting for transfers between devices: 500 us -> none  [the longest x1 140 us: per_device(): lax.psum_scatter(g_node_in, ('slab', 'lat'), scatter_dimension=0, tiled=T...]
    all_gather x3 -> x0, blocking collectives: 168 us -> none  [the longest x1 79.1 us: per_device(): lax.all_gather(w_edge_out, ('slab', 'lat'), axis=0, tiled=True)]
    pallas_call x0 -> x1, Pallas kernels: none -> 129 us  [per_device(): pl.pallas_call(functools.partial(layer_kernel, slab_bits, lat_bits, [*inp...]
    dot_general x12 -> x0, matrix products: 18.7 us -> none  [the longest x4 10.1 us: contract_rows(): lax.dot_general(left, right, (((0,), (0,)), ((), ())), preferred_element_...]
    scatter-add x5 -> x0, other arithmetic: 17.7 us -> none  [the longest x1 6.51 us: per_device(): d_extended = d_extended.at[halo_rows + dst_row].add(d_joined[:, 2 * L:])]
    unnamed x10 -> x0, waiting for transfers between devices: 13.5 us -> none
    gather x6 -> x0, local copies, waits for them, and re-layouts: 11.7 us -> none  [the longest x2 2.94 us: pick_blocks(): jnp.take(source_table.reshape(-1, BLK, width), blocks, axis=0)]
    all_gather x3 -> x0, waiting for transfers between devices: 9.72 us -> none  [the longest x1 9.7 us: per_device(): lax.all_gather(w_node_in, ('slab', 'lat'), axis=0, tiled=True)]
  transfers between devices with their start and end apart: 15 -> 0, of which waited for: 7 -> 0; matrix products, arithmetic and copies ran while one was open for 5% -> 0% of each run, Pallas kernels for 0% -> 0%
where the time goes in v2:
time: 139 us; the launch traced here: 138 us
  Pallas kernels  129 us (93%)
  local copies, waits for them, and re-layouts  8.11 us (6%)
    pallas_call x1, Pallas kernels, per_device(): pl.pallas_call(functools.partial(layer_kernel, slab_bits, lat_bits, [*inp...  129 us
    unnamed x20, local copies, waits for them, and re-layouts  8.11 us

profile of v2, /device:TPU:0, one launch (start us, length us, event | category | flops | bytes accessed | tf_op | source)
XLA Modules:
  0.0 138.2 jit_solution(13540073719105198926)
XLA Ops:
  1.3 128.8 %mesh_layer.1 = (bf16[4,128,128]{2,1,0:T(8,128)(2,1)}, bf16[512,512]{1,0:T(8,128)(2,1)}, bf16[512,128]{1,0:T(8,128)(2,1)}, bf16[512,512]{1,0:T(8,128)(2,1)}, f32...) custom-call(bf16[512,128]{1,0:T(8,128)(2,1)} %refs_0_.1, ...), custom_call_target="tpu_custom_call" | custom-call | tf_op jit(solution)/shard_map/mesh_layer/pallas_call | solution.py:625
  130.1 1.6 %copy.31 = bf16[512,128]{1,0:T(8,128)(2,1)} copy(bf16[512,128]{1,0:T(8,128)(2,1)} %bitcast.3) | data formatting | bytes 262144
  131.7 0.0 copy-start.1
  131.7 0.0 copy-start
  131.7 1.9 %copy.32 = bf16[512,512]{1,0:T(8,128)(2,1)} copy(bf16[512,512]{1,0:T(8,128)(2,1)} %get-tuple-element.33) | data formatting | bytes 1048576
  133.6 0.0 copy-done.1
  133.6 0.7 copy.33
  134.2 0.0 copy-done
  134.3 0.0 copy-start.2
  134.3 0.8 copy.34
  135.0 0.2 copy-done.2
  135.2 0.0 copy-start.5
  135.2 0.6 copy.35
  135.9 0.1 copy-done.5
  136.0 0.0 copy-start.3
  136.0 0.6 copy.36
  136.6 0.2 copy-done.3
  136.8 0.0 copy-start.4
  136.8 0.6 copy.37
  137.5 0.1 copy-done.4
  137.6 0.6 copy.38
Async XLA Ops:
  131.7 1.9 %copy-start.1 = (bf16[512,128]{1,0:T(8,128)(2,1)S(1)}, bf16[512,128]{1,0:T(8,128)(2,1)}, u32[]{:S(2)}) copy-start(bf16[512,128]{1,0:T(8,128)(2,1)} %get-tuple-element.34) | copy-start | bytes 393220
  131.7 2.6 %copy-start = (bf16[512,512]{1,0:T(8,128)(2,1)S(1)}, bf16[512,512]{1,0:T(8,128)(2,1)}, u32[]{:S(2)}) copy-start(bf16[512,512]{1,0:T(8,128)(2,1)} %get-tuple-element.35) | copy-start | bytes 1572868
  134.3 1.0 copy-start.2
  135.2 0.8 copy-start.5
  136.0 0.9 copy-start.3
  136.8 0.8 copy-start.4

commit v3 on v2

--- a/solution.py
+++ b/solution.py
@@ -220,6 +220,8 @@
 
     r.recv_hot[...] = places(0, slab_rows)
     r.send_hot[...] = places(1, all_rows)
+    r.recv_turned[...] = r.recv_hot[...].T
+    r.send_turned[...] = r.send_hot[...].T
     chunk = 2 * BLK
     parts = edge_rows // chunk
 
@@ -296,9 +298,9 @@
         ext[halo_rows + slab_rows :, cols] = up[t]
     joined = r.joined
     joined[0] = r.edges[...]
-    joined[1] = contract_rows(r.send_hot[...], ext[...]).astype(bf16)
-    joined[2] = contract_rows(
-        r.recv_hot[...], ext[halo_rows : halo_rows + slab_rows, :]
+    joined[1] = dot(r.send_turned[...], ext[...]).astype(bf16)
+    joined[2] = dot(
+        r.recv_turned[...], ext[halo_rows : halo_rows + slab_rows, :]
     ).astype(bf16)
     gather_step(edge_pieces, steps - 1)
     gather_step(node_pieces, steps - 3)
@@ -339,6 +341,9 @@
             begin(remote(r.node_cotangent.at[rows], cot.at[lat], {"lat": peer(k)}))
         )
     cot[lat] = r.node_cotangent[pl.ds(pl.multiple_of(lat * own_rows, own_rows), own_rows), :]
+    for k in range(3):
+        r.joined_turned[k] = joined[k].T
+    r.first_turned[...] = r.first[...].T
     gather_step(node_pieces, steps - 1)
     node_in[...], node_out[...] = whole(2), whole(3)
     own_latents = ext[pl.ds(pl.multiple_of(halo_rows + lat * own_rows, own_rows), own_rows), :]
@@ -432,8 +437,8 @@
 
     for copy in agg_copies:
         copy.wait_recv()
-    r.d_edge[...] = contract_rows(
-        r.recv_hot[...], d_agg[...].reshape(slab_rows, L)
+    r.d_edge[...] = dot(
+        r.recv_turned[...], d_agg[...].reshape(slab_rows, L)
     ).astype(bf16)
 
     def edge_second(n, carry):
@@ -446,7 +451,7 @@
         return carry
 
     lax.fori_loop(0, parts, edge_second, 0)
-    put_grad(1, contract_rows(r.first[...], r.top[...]))
+    put_grad(1, dot(r.first_turned[...], r.top[...]))
     for p in node_pieces:
         scatter_step(p, 1)
 
@@ -464,13 +469,13 @@
         r.grad_edges[rows, :] = (
             r.edge_cotangent[rows, :].astype(f32) + direct
         ).astype(bf16)
-        r.far[rows, :] = times_transpose(d_first, edge_in[L : 2 * L, :]).astype(bf16)
+        r.first[rows, :] = times_transpose(d_first, edge_in[L : 2 * L, :]).astype(bf16)
         r.d_edge[rows, :] = times_transpose(d_first, edge_in[2 * L :, :]).astype(bf16)
         return carry
 
     lax.fori_loop(0, parts, edge_joined, 0)
     d_ext = r.d_ext
-    d_ext[...] = dot(r.send_hot[...], r.far[...])
+    d_ext[...] = dot(r.send_hot[...], r.first[...])
     d_ext[halo_rows : halo_rows + slab_rows, :] += dot(r.recv_hot[...], r.d_edge[...])
     mine = pl.ds(pl.multiple_of(halo_rows + lat * own_rows, own_rows), own_rows)
     d_ext[mine, :] += d_direct
@@ -481,7 +486,7 @@
     )
     put_grad(
         0,
-        jnp.concatenate([contract_rows(joined[k], r.rest[...]) for k in range(3)], axis=0),
+        jnp.concatenate([dot(r.joined_turned[k], r.rest[...]) for k in range(3)], axis=0),
     )
     arrive()
     for block in range(slab_rows // BLK):
@@ -517,6 +522,30 @@
         copy.wait_send()
     leave_latents()
     leave_grads()
+
+
+def hand_out_kernel(*refs):
+    sem = refs[-1]
+    half = (len(refs) - 1) // 2
+    copies = [
+        pltpu.make_async_copy(refs[n], refs[half + n], sem.at[n]) for n in range(half)
+    ]
+    for copy in copies:
+        copy.start()
+    for copy in copies:
+        copy.wait()
+
+
+def hand_out(results):
+    return pl.pallas_call(
+        hand_out_kernel,
+        out_shape=[jax.ShapeDtypeStruct(v.shape, v.dtype) for v in results],
+        in_specs=[pl.BlockSpec(memory_space=pl.ANY)] * len(results),
+        out_specs=[pl.BlockSpec(memory_space=pl.ANY)] * len(results),
+        scratch_shapes=[pltpu.SemaphoreType.DMA((len(results),))],
+        compiler_params=pltpu.CompilerParams(vmem_limit_bytes=60 * 1024 * 1024),
+        name="hand_out",
+    )(*results)
 
 
 def per_device(
@@ -584,6 +613,10 @@
         send_hot=((all_rows, edge_rows), bf16),
         ext=((all_rows, L), bf16),
         joined=((3, edge_rows, L), bf16),
+        recv_turned=((edge_rows, slab_rows), bf16),
+        send_turned=((edge_rows, all_rows), bf16),
+        joined_turned=((3, L, edge_rows), bf16),
+        first_turned=((L, edge_rows), bf16),
         first=((edge_rows, L), bf16),
         normed=((edge_rows, L), f32),
         inverse=((edge_rows, 1), f32),
@@ -601,7 +634,6 @@
         back_up=((halo_rows, L), bf16),
         from_below=((halo_rows, L), bf16),
         from_above=((halo_rows, L), bf16),
-        far=((edge_rows, L), bf16),
         mat0=((whole_rows[0], L), bf16),
         mat1=((whole_rows[1], L), bf16),
         mat2=((whole_rows[2], L), bf16),
@@ -635,11 +667,11 @@
         scratch_shapes=[pltpu.VMEM(*s) for s in shapes]
         + [pltpu.SemaphoreType.DMA((copies,)), pltpu.SemaphoreType.DMA((copies,))],
         compiler_params=pltpu.CompilerParams(
-            collective_id=0, has_side_effects=True, vmem_limit_bytes=56 * 1024 * 1024
+            collective_id=0, has_side_effects=True, vmem_limit_bytes=58 * 1024 * 1024
         ),
         name="mesh_layer",
     )(*inputs.values())
-    return (results[0].reshape(nodes.shape), *results[1:])
+    return tuple(hand_out((results[0].reshape(nodes.shape), *results[1:])))
 
 
 def solution(mesh):

time: 139 us -> 178 us (1.28)
  Pallas kernels: 129 us -> 177 us
  local copies, waits for them, and re-layouts: 8.11 us -> 0 us
    pallas_call x0 -> x1, Pallas kernels: none -> 47.8 us  [hand_out(): pl.pallas_call(hand_out_kernel, out_shape=[jax.ShapeDtypeStruct(v.shape,...]
    unnamed x20 -> x0, local copies, waits for them, and re-layouts: 8.11 us -> none
where the time goes in v3:
time: 178 us
  Pallas kernels  177 us (99%)
    pallas_call x1, Pallas kernels, per_device(): pl.pallas_call(functools.partial(layer_kernel, slab_bits, lat_bits, [*inp...  129 us
    pallas_call x1, Pallas kernels, hand_out(): pl.pallas_call(hand_out_kernel, out_shape=[jax.ShapeDtypeStruct(v.shape,...  47.8 us

profile of v3, /device:TPU:0, one launch (start us, length us, event | category | flops | bytes accessed | tf_op | source)
XLA Modules:
  0.0 177.9 jit_solution(2725303983688740943)
XLA Ops:
  1.3 128.8 %mesh_layer.1 = (bf16[4,128,128]{2,1,0:T(8,128)(2,1)}, bf16[512,512]{1,0:T(8,128)(2,1)}, bf16[512,128]{1,0:T(8,128)(2,1)}, bf16[512,512]{1,0:T(8,128)(2,1)}, f32...) custom-call(bf16[512,128]{1,0:T(8,128)(2,1)} %refs_0_.1, ...), custom_call_target="tpu_custom_call" | custom-call | tf_op jit(solution)/shard_map/mesh_layer/pallas_call | solution.py:657
  130.1 47.8 %hand_out.1 = (bf16[512,128]{1,0:T(8,128)(2,1)}, bf16[512,512]{1,0:T(8,128)(2,1)}, bf16[512,128]{1,0:T(8,128)(2,1)}, bf16[512,512]{1,0:T(8,128)(2,1)}, f32[48,51...) custom-call(bf16[512,128]{1,0:T(8,128)(2,1)} %bitcast.3, ...), custom_call_target="tpu_custom_call" | custom-call | tf_op jit(solution)/shard_map/hand_out/pallas_call | solution.py:540
